TPU v7x, 512 devices: a whole 4x8x8 slice. The times are simulated.
512 devices in a mesh: ka: 64 (over z, x, y_lo), ta: 8 (over y_hi, core).
Axes of the slice: x: 4, y: 8 (y_hi: 4, y_lo: 2; y = y_hi * 2 + y_lo), z: 8, core: 2. Of those that a mesh axis runs over, the one named last changes fastest.
Arguments:
- green_time: bfloat16 [2048, 256, 256], P(('ta', 'ka')), parts along dimension 0, may hold values from -0.375 to 0.375
- orbitals: bfloat16 [256, 256, 512], P('ka'), may hold values from -3.296875 to 3.296875
- pair_table: int32 [256, 256], P(None, 'ka'), may hold values from 0 to 255, as said below
- pair_momenta: int32 [2], replicated, may hold values from 0 to 255
- owner_rows: int32 [512], replicated, may hold values from 0 to 511, each once
Outputs:
- bubble: float32 [4096, 2, 512], P(('ta', 'ka')), parts along dimension 0
There are 8 independent parts, one for each index of `ta`. A program takes and returns all parts, laid end to end along the dimension named above; an argument that names none is the same for every part. Nothing has to cross between parts.
Inputs may be any that keep to these rules, and one draw needn't show every extreme that they name: The momenta form a 4 x 4 x (16) periodic lattice listed in an order drawn from the seed; row a of pair_table gives, for each k, the index of momentum a minus momentum k, so every row is a permutation of 0 to 255.
All inputs are finite; a program needn't handle non-finite values.
Results may differ from a plain program's by a relative error of at most 0.0057.
Values may be sent and summed in bfloat16 or wider, within the bound.
A program may use at most 64 MiB of HBM per device.

v0:
```python
import jax
import jax.numpy as jnp
from jax import lax
from jax.sharding import PartitionSpec as P


def per_device(green_time, orbitals, pair_table, pair_momenta, owner_rows):
    orbitals_owned = jnp.take(orbitals, owner_rows, axis=2)
    half_product = jnp.einsum(
        "kij,kjp->kip", green_time, orbitals, preferred_element_type=jnp.float32
    ).astype(jnp.bfloat16)
    projected = jnp.einsum(
        "kia,kip->kap", orbitals_owned, half_product, preferred_element_type=jnp.float32
    ).astype(jnp.bfloat16)
    local_pairs = jnp.take(pair_table, pair_momenta, axis=0)
    partners = lax.all_gather(local_pairs, "ka", axis=1, tiled=True)
    inverse_count = 1.0 / partners.shape[1]
    spread = lax.all_to_all(projected, "ka", split_axis=1, concat_axis=0, tiled=True)
    partner_blocks = jnp.take(spread, partners, axis=0)
    returned = lax.all_to_all(partner_blocks, "ka", split_axis=1, concat_axis=2, tiled=True)
    return lax.psum_scatter(
        jnp.einsum("kac,qkac->aqc", projected, returned, preferred_element_type=jnp.float32)
        * inverse_count,
        "ka",
        scatter_dimension=0,
        tiled=True,
    )


def solution(mesh):
    return jax.shard_map(
        per_device,
        mesh=mesh,
        in_specs=(P(("ta", "ka"), None, None), P("ka", None, None), P(None, "ka"), P(), P()),
        out_specs=P(("ta", "ka"), None, None),
        check_vma=False,
    )
```

profile of v0, /device:TPU:16, one launch (start us, length us, event | category | flops | bytes accessed | tf_op | source)
XLA Modules:
  0.0 922.7 jit_solution(13758151225031022009)
XLA Ops:
  6.5 0.7 compare_select_fusion.1
  7.3 0.7 compare_and_fusion.1
  8.0 1.7 copy.32
  9.7 2.4 gather_fusion.1
  12.1 2.7 select_bitcast_fusion
  14.7 4.5 bitcast_convert_fusion
  19.2 2.9 copy.34
  22.1 14.8 %all-to-all-start = ((bf16[4,512,512]{2,0,1:T(4,128)(2,1)}), bf16[4,512,512]{2,0,1:T(4,128)(2,1)S(1)}, u32[]{:S(2)}, u32[]{:S(2)}) async-start(bf16[4,512,512]{2,0,1:T(4,128)(2,1)} %copy.34), calls=%async_computation | async-start | bytes 4194304 | tf_op jit(solution)/shard_map/all_to_all | solution.py:18
  37.0 0.1 copy.29
  37.2 0.6 gather_fusion
  37.8 173.9 %all-gather = s32[64,4,2]{1,2,0:T(2,128)S(1)} all-gather(s32[1,4,2]{1,2,0:T(2,128)S(1)} %select_bitcast_fusion.1), channel_id=1, replica_groups=mesh['ka'=64,'ta'=8] {'ka'}, dimensions={0}, use_global_device_ids=true | all-gather | bytes 2080 | tf_op jit(solution)/shard_map/all_gather | solution.py:16
  211.7 0.1 reshape.44
  211.9 0.2 copy.31
  212.1 0.4 copy.61
  212.5 0.3 copy.36
  212.8 3.5 gather_fusion.2
  216.3 2.6 copy_select_fusion
  218.9 73.9 %all_to_all.36 = bf16[2,256,8,512]{3,2,0,1:T(8,128)(2,1)S(1)} all-to-all(bf16[2,256,8,512]{3,2,0,1:T(8,128)(2,1)S(1)} %copy_select_fusion), channel_id=1, replica_groups=mesh['ka'=64,'ta'=8] {'ka'}, dimensions={1} | all-to-all | bytes 8388608 | tf_op jit(solution)/shard_map/all_to_all | solution.py:20
  292.7 1.2 multiply_reduce_fusion
  293.9 0.2 broadcast_multiply_fusion
  294.1 2.9 copy.60
  297.1 1.3 dynamic-slice
  299.0 615.5 %all-reduce.3.cloned.1.call-done = f32[512,2,512]{2,1,0:T(2,128)} async-done(((f32[512,2,512]{2,1,0:T(2,128)}), f32[512,2,512]{2,1,0:T(2,128)}) %all-reduce.3.cloned.1.call-update) | async-done | bytes 2097168
  914.5 1.4 constant_dynamic-slice_fusion
  (21 shorter events, 0.2 us)
Async XLA Ops:
  6.5 8.2 copy-start
  19.2 17.8 %copy-start.2 = (s32[256,4]{0,1:T(4,128)S(1)}, s32[256,4]{0,1:T(4,128)}, u32[]{:S(2)}) copy-start(s32[256,4]{0,1:T(4,128)} %param.7) | copy-start | bytes 12292
  19.2 18.0 %copy-start.3 = (s32[2]{0:T(128)S(1)}, s32[2]{0:T(128)}, u32[]{:S(2)}) copy-start(s32[2]{0:T(128)} %param.8) | copy-start | bytes 28
  22.1 189.9 %all-to-all-start = ((bf16[4,512,512]{2,0,1:T(4,128)(2,1)}), bf16[4,512,512]{2,0,1:T(4,128)(2,1)S(1)}, u32[]{:S(2)}, u32[]{:S(2)}) async-start(bf16[4,512,512]{2,0,1:T(4,128)(2,1)} %copy.34), calls=%async_computation | async-start | bytes 4194304 | tf_op jit(solution)/shard_map/all_to_all | solution.py:18
  36.9 877.5 %all-reduce.3.cloned.1.call-start = ((), (), s32[]{:S(2)}) async-start(), calls=%async_computation.2 | async-start | bytes 4194304
  218.9 73.9 %copy-start.1 = (f32[512,512,4]{1,0,2:T(8,128)S(1)}, f32[512,512,4]{1,0,2:T(8,128)}, u32[]{:S(2)}) copy-start(f32[512,512,4]{1,0,2:T(8,128)} %get-tuple-element.5) | copy-start | bytes 12582916
Sparse Core Ops, SparseCore 0:
  297.2 617.2 all-reduce.2
where the time goes:
time: 923 us
  waiting for transfers between devices  615 us (67%)
  blocking collectives  248 us (27%)
  local copies, waits for them, and re-layouts  17.7 us (2%)
  starting transfers between devices  14.8 us (2%)
  between operations  14.2 us (2%)
    unnamed x2, waiting for transfers between devices  615 us
    all_gather x1, blocking collectives, per_device(): partners = lax.all_gather(local_pairs, 'ka', axis=1, tiled=True)  174 us
    all_to_all x1, blocking collectives, per_device(): lax.all_to_all(partner_blocks, 'ka', split_axis=1, concat_axis=2, tiled=T...  73.9 us
  transfers between devices with their start and end apart: 2, of which 1 were waited for; matrix products, arithmetic and copies ran while one was open for 0% of the time, Pallas kernels for 0%

commit v1 on v0

--- a/solution.py
+++ b/solution.py
@@ -13,7 +13,10 @@
         "kia,kip->kap", orbitals_owned, half_product, preferred_element_type=jnp.float32
     ).astype(jnp.bfloat16)
     local_pairs = jnp.take(pair_table, pair_momenta, axis=0)
-    partners = lax.all_gather(local_pairs, "ka", axis=1, tiled=True)
+    count = lax.axis_size("ka")
+    blocks = jnp.stack([local_pairs for _ in range(count)])
+    blocks = lax.all_to_all(blocks, "ka", split_axis=0, concat_axis=0)
+    partners = jnp.concatenate(blocks, axis=1)
     inverse_count = 1.0 / partners.shape[1]
     spread = lax.all_to_all(projected, "ka", split_axis=1, concat_axis=0, tiled=True)
     partner_blocks = jnp.take(spread, partners, axis=0)

time: 923 us -> 843 us (0.913)
  blocking collectives: 248 us -> 103 us
  waiting for transfers between devices: 615 us -> 665 us
  starting transfers between devices: 14.8 us -> 26 us
    all_gather x1 -> x0, blocking collectives: 174 us -> none  [per_device(): partners = lax.all_gather(local_pairs, 'ka', axis=1, tiled=True)]
    all_to_all x1, waiting for transfers between devices: 0.01 us -> 49.4 us  [per_device(): lax.all_to_all(projected, 'ka', split_axis=1, concat_axis=0, tiled=True)]
    all_to_all x1, blocking collectives: 73.9 us -> 103 us  [per_device(): lax.all_to_all(partner_blocks, 'ka', split_axis=1, concat_axis=2, tiled=T...]
    all_to_all x0 -> x1, starting transfers between devices: none -> 14.8 us  [per_device(): blocks = lax.all_to_all(blocks, 'ka', split_axis=0, concat_axis=0)]
  transfers between devices with their start and end apart: 2 -> 3, of which waited for: 1 -> 2; matrix products, arithmetic and copies ran while one was open for 0% -> 2% of each run, Pallas kernels for 0% -> 0%
where the time goes in v1:
time: 843 us; the launch traced here: 842 us
  waiting for transfers between devices  665 us (79%)
  blocking collectives  103 us (12%)
  starting transfers between devices  26 us (3%)
  local copies, waits for them, and re-layouts  19.2 us (2%)
  between operations  14.2 us (2%)
  other arithmetic  9.49 us (1%)
    unnamed x2, waiting for transfers between devices  616 us
    all_to_all x1, blocking collectives, per_device(): lax.all_to_all(partner_blocks, 'ka', split_axis=1, concat_axis=2, tiled=T...  103 us
    all_to_all x1, waiting for transfers between devices, per_device(): lax.all_to_all(projected, 'ka', split_axis=1, concat_axis=0, tiled=True)  49.4 us
  transfers between devices with their start and end apart: 3, of which 2 were waited for; matrix products, arithmetic and copies ran while one was open for 2% of the time, Pallas kernels for 0%

profile of v1, /device:TPU:16, one launch (start us, length us, event | category | flops | bytes accessed | tf_op | source)
XLA Modules:
  0.0 842.1 jit_solution(17705653232876483384)
XLA Ops:
  6.5 0.7 compare_select_fusion.3
  7.3 0.7 compare_and_fusion.2
  7.9 0.8 copy.27
  8.7 0.6 gather_fusion
  9.4 0.7 stack.2
  10.0 14.8 %all-to-all-start = ((s32[64,2,4]{2,1,0:T(2,128)}), s32[64,2,4]{2,1,0:T(2,128)S(1)}, u32[]{:S(2)}, u32[]{:S(2)}) async-start(s32[64,2,4]{2,1,0:T(2,128)} %stack.2), calls=%async_computation | async-start | bytes 131072 | tf_op jit(solution)/shard_map/all_to_all | solution.py:18
  24.8 0.7 compare_select_fusion.2
  25.5 0.7 compare_and_fusion.1
  26.2 1.7 copy.30
  27.9 2.4 gather_fusion.1
  30.3 2.7 select_bitcast_fusion
  33.0 4.5 bitcast_convert_fusion
  37.4 2.9 copy.32
  40.4 11.2 %all-to-all-start.1 = ((bf16[4,512,512]{2,0,1:T(4,128)(2,1)}), bf16[4,512,512]{2,0,1:T(4,128)(2,1)S(1)}, u32[]{:S(2)}, u32[]{:S(2)}) async-start(bf16[4,512,512]{2,0,1:T(4,128)(2,1)} %copy.32), calls=%async_computation.1 | async-start | bytes 4194304 | tf_op jit(solution)/shard_map/all_to_all | solution.py:21
  52.1 49.4 %all-to-all-done.1 = bf16[4,512,512]{2,0,1:T(4,128)(2,1)S(1)} async-done(((bf16[4,512,512]{2,0,1:T(4,128)(2,1)}), bf16[4,512,512]{2,0,1:T(4,128)(2,1)S(1)}, u32[]{:S(2)}, u32[]{:S(2)}) %all-to-all-start.1) | async-done | bytes 2097184 | tf_op jit(solution)/shard_map/all_to_all | solution.py:21
  101.5 0.4 copy.60
  102.2 3.5 gather_fusion.2
  105.7 2.6 copy_select_fusion
  108.3 103.4 %all_to_all.41 = bf16[2,256,8,512]{3,2,0,1:T(8,128)(2,1)S(1)} all-to-all(bf16[2,256,8,512]{3,2,0,1:T(8,128)(2,1)S(1)} %copy_select_fusion), channel_id=1, replica_groups=mesh['ka'=64,'ta'=8] {'ka'}, dimensions={1} | all-to-all | bytes 8388608 | tf_op jit(solution)/shard_map/all_to_all | solution.py:23
  211.7 1.2 multiply_reduce_fusion
  213.1 2.9 copy.59
  216.1 1.3 dynamic-slice
  218.0 615.9 %all-reduce.3.cloned.1.call-done = f32[512,2,512]{2,1,0:T(2,128)} async-done(((f32[512,2,512]{2,1,0:T(2,128)}), f32[512,2,512]{2,1,0:T(2,128)}) %all-reduce.3.cloned.1.call-update) | async-done | bytes 2097168
  833.9 1.4 constant_dynamic-slice_fusion
  (20 shorter events, 1.1 us)
Async XLA Ops:
  6.5 26.4 %copy-start = (bf16[4,256,256]{2,1,0:T(8,128)(2,1)S(1)}, bf16[4,256,256]{2,1,0:T(8,128)(2,1)}, u32[]{:S(2)}) copy-start(bf16[4,256,256]{2,1,0:T(8,128)(2,1)} %param.5) | copy-start | bytes 1572868
  10.0 30.3 %all-to-all-start = ((s32[64,2,4]{2,1,0:T(2,128)}), s32[64,2,4]{2,1,0:T(2,128)S(1)}, u32[]{:S(2)}, u32[]{:S(2)}) async-start(s32[64,2,4]{2,1,0:T(2,128)} %stack.2), calls=%async_computation | async-start | bytes 131072 | tf_op jit(solution)/shard_map/all_to_all | solution.py:18
  40.4 61.1 %all-to-all-start.1 = ((bf16[4,512,512]{2,0,1:T(4,128)(2,1)}), bf16[4,512,512]{2,0,1:T(4,128)(2,1)S(1)}, u32[]{:S(2)}, u32[]{:S(2)}) async-start(bf16[4,512,512]{2,0,1:T(4,128)(2,1)} %copy.32), calls=%async_computation.1 | async-start | bytes 4194304 | tf_op jit(solution)/shard_map/all_to_all | solution.py:21
  51.6 782.3 %all-reduce.3.cloned.1.call-start = ((), (), s32[]{:S(2)}) async-start(), calls=%async_computation.3 | async-start | bytes 4194304
  108.3 103.4 %copy-start.1 = (f32[512,512,4]{1,0,2:T(8,128)S(1)}, f32[512,512,4]{1,0,2:T(8,128)}, u32[]{:S(2)}) copy-start(f32[512,512,4]{1,0,2:T(8,128)} %get-tuple-element.5) | copy-start | bytes 12582916
Sparse Core Ops, SparseCore 0:
  216.2 617.6 all-reduce.2
